TPU v7x, 32 devices: a whole 2x2x4 slice. The times are simulated.
32 devices in a mesh: rows: 8 (over z, y), snaps: 4 (over x, core).
Axes of the slice: x: 2, y: 2, z: 4, core: 2. Of those that a mesh axis runs over, the one named last changes fastest.
Arguments:
- stress: float32 [131072, 1024], P('rows', 'snaps'), may hold values from -80 to 80
- sketch: float32 [64, 1024], P(None, 'snaps'), may hold values from -0.1875 to 0.1875
Outputs:
- basis: float32 [64, 131072], P(None, ('rows', 'snaps'))
- coeffs: float32 [64, 1024], P(None, 'snaps')
- spectrum: float32 [64, 64], replicated
All inputs are finite; a program needn't handle non-finite values.
Results may differ from a plain program's by a relative error of at most 0.0015.
Values sent between devices are 32-bit elements; how exact they have to be, the bound alone decides.
A program may use at most 128 MiB of HBM per device.

v0:
```python
import math
import jax
import jax.numpy as jnp
from jax import lax
from jax.sharding import PartitionSpec as P


def product(left_m, right_m, left_dim, right_dim):
    return lax.dot_general(
        left_m,
        right_m,
        (((left_dim,), (right_dim,)), ((), ())),
        precision=lax.Precision.HIGHEST,
        preferred_element_type=jnp.float32,
    )


def inverse_factor(gram_total):
    lower = jnp.linalg.cholesky(gram_total)
    ident = jnp.eye(gram_total.shape[0], dtype=gram_total.dtype)
    return lax.linalg.triangular_solve(lower, ident, left_side=True, lower=True)


def section_whole(panel, stress):
    factor = inverse_factor(lax.psum(product(panel, panel, 1, 1), "rows"))
    basis = product(factor, panel, 1, 0)
    coeffs = lax.psum(product(basis, stress, 1, 0), "rows")
    return (basis, coeffs)


def on_device(stress, sketch):
    rows_dev = stress.shape[0]
    groups = lax.axis_size("snaps")
    share = rows_dev // groups
    operand = sketch
    basis = None
    for turn in range(2):
        partial_value = product(operand, stress, 1, 1)
        panel = lax.psum(partial_value, "snaps")
        basis, operand = section_whole(panel, stress)
    basis = lax.dynamic_slice_in_dim(basis, lax.axis_index("snaps") * share, share, 1)
    scale = math.sqrt(float(rows_dev * lax.axis_size("rows")))
    batch_total = operand.shape[1] * groups
    spectrum = lax.psum(product(operand, operand, 1, 1), "snaps") / batch_total
    return (basis * scale, operand, spectrum)


def solution(mesh):
    placed = (P("rows", "snaps"), P(None, "snaps"))
    return jax.shard_map(
        on_device,
        mesh=mesh,
        in_specs=placed,
        out_specs=(P(None, ("rows", "snaps")), P(None, "snaps"), P()),
        check_vma=False,
    )
```

profile of v0, /device:TPU:0, one launch (start us, length us, event | category | flops | bytes accessed | tf_op | source)
XLA Modules:
  0.0 522.6 jit_solution(17021512674975102727)
XLA Ops:
  7.2 0.0 copy-start
  7.2 0.0 all-reduce.5.cloned.1.call-start
  7.2 0.8 copy-done
  8.0 20.6 %fusion.12 = f32[64,16384]{1,0:T(8,128)} fusion(f32[64,256]{1,0:T(8,128)S(1)} %copy-done, f32[16384,256]{1,0:T(8,128)} %param.5), kind=kOutput, calls=%fused_computation.23 | convolution fusion | flops 3221225472 | bytes 21037056 | tf_op jit(solution)/shard_map/dot_general | solution.py:9
  28.6 0.0 all-reduce.5.cloned.1.call-update
  28.7 0.0 all-reduce.7.cloned.1.call-start
  28.7 88.3 %all-reduce.5.cloned.1.call-done = f32[64,16384]{1,0:T(8,128)} async-done(((f32[64,16384]{1,0:T(8,128)}), f32[64,16384]{1,0:T(8,128)}) %all-reduce.5.cloned.1.call-update) | async-done | bytes 4194320 | tf_op jit(solution)/shard_map/psum | solution.py:39
  117.0 6.9 %fusion.13 = f32[64,64]{0,1:T(8,128)S(1)} fusion(f32[64,16384]{1,0:T(8,128)} %all-reduce.5.cloned.1.call-done), kind=kOutput, calls=%fused_computation.24 | convolution fusion | flops 805306368 | bytes 4210688 | tf_op jit(solution)/shard_map/dot_general | solution.py:9
  124.0 37.2 %psum.50 = f32[64,64]{0,1:T(8,128)S(1)} all-reduce(f32[64,64]{0,1:T(8,128)S(1)} %fusion.13), channel_id=1, replica_groups=mesh['rows'=8,'snaps'=4] {'rows'}, use_global_device_ids=true, to_apply=%region_1.0 | all-reduce | flops 4096 | bytes 32768 | tf_op jit(solution)/shard_map/psum | solution.py:25
  161.1 0.1 copy.6
  161.2 5.8 %cholesky.44 = f32[64,64]{1,0:T(8,128)S(1)} custom-call(f32[64,64]{1,0:T(8,128)S(1)} %fusion.9), custom_call_target="Cholesky" | custom-call | tf_op jit(solution)/shard_map/jit(cholesky)/cholesky | solution.py:19
  167.1 0.6 compare_reduce_fusion.1
  167.7 0.7 fusion.4
  168.4 4.9 custom-call.6
  173.3 0.3 fusion.2
  173.5 5.5 %fusion.14 = f32[64,16384]{1,0:T(8,128)S(1)} fusion(f32[64,64]{1,0:T(8,128)S(1)} %fusion.2, f32[64,16384]{1,0:T(8,128)} %all-reduce.5.cloned.1.call-done), kind=kOutput, calls=%fused_computation.25 | convolution fusion | flops 805306368 | bytes 8404992 | tf_op jit(solution)/shard_map/dot_general | solution.py:9
  179.0 11.6 %fusion.15 = f32[64,256]{1,0:T(8,128)} fusion(f32[64,16384]{1,0:T(8,128)S(1)} %fusion.14, f32[16384,256]{1,0:T(8,128)} %param.5), kind=kOutput, calls=%fused_computation.26 | convolution fusion | flops 3221225472 | bytes 21037056 | tf_op jit(solution)/shard_map/dot_general | solution.py:9
  190.6 0.0 all-reduce.7.cloned.1.call-update
  190.6 0.3 all-reduce.9.cloned.1.call-start
  190.9 64.8 %all-reduce.7.cloned.1.call-done = f32[64,256]{1,0:T(8,128)} async-done(((f32[64,256]{1,0:T(8,128)}), f32[64,256]{1,0:T(8,128)}) %all-reduce.7.cloned.1.call-update) | async-done | bytes 65552 | tf_op jit(solution)/shard_map/psum | solution.py:27
  255.7 20.6 %fusion.16 = f32[64,16384]{1,0:T(8,128)} fusion(f32[64,256]{1,0:T(8,128)} %all-reduce.7.cloned.1.call-done, f32[16384,256]{1,0:T(8,128)} %param.5), kind=kOutput, calls=%fused_computation.27 | convolution fusion | flops 3221225472 | bytes 21037056 | tf_op jit(solution)/shard_map/dot_general | solution.py:9
  276.3 0.0 all-reduce.9.cloned.1.call-update
  276.4 0.0 all-reduce.11.cloned.1.call-start
  276.4 85.5 %all-reduce.9.cloned.1.call-done = f32[64,16384]{1,0:T(8,128)} async-done(((f32[64,16384]{1,0:T(8,128)}), f32[64,16384]{1,0:T(8,128)}) %all-reduce.9.cloned.1.call-update) | async-done | bytes 4194320 | tf_op jit(solution)/shard_map/psum | solution.py:39
  361.9 6.9 %fusion.17 = f32[64,64]{0,1:T(8,128)S(1)} fusion(f32[64,16384]{1,0:T(8,128)} %all-reduce.9.cloned.1.call-done), kind=kOutput, calls=%fused_computation.28 | convolution fusion | flops 805306368 | bytes 4210688 | tf_op jit(solution)/shard_map/dot_general | solution.py:9
  368.9 37.1 %psum.53 = f32[64,64]{0,1:T(8,128)S(1)} all-reduce(f32[64,64]{0,1:T(8,128)S(1)} %fusion.17), channel_id=1, replica_groups=mesh['rows'=8,'snaps'=4] {'rows'}, use_global_device_ids=true, to_apply=%region_6.9 | all-reduce | flops 4096 | bytes 32768 | tf_op jit(solution)/shard_map/psum | solution.py:25
  406.0 0.1 copy.8
  406.1 5.8 %cholesky.55 = f32[64,64]{1,0:T(8,128)S(1)} custom-call(f32[64,64]{1,0:T(8,128)S(1)} %fusion.7), custom_call_target="Cholesky" | custom-call | tf_op jit(solution)/shard_map/jit(cholesky)/cholesky | solution.py:19
  412.0 0.6 compare_reduce_fusion
  412.7 0.7 fusion.5
  413.3 4.9 custom-call.7
  418.2 0.3 fusion
  418.5 5.5 %fusion.18 = f32[64,16384]{1,0:T(8,128)S(1)} fusion(f32[64,64]{1,0:T(8,128)S(1)} %fusion, f32[64,16384]{1,0:T(8,128)} %all-reduce.9.cloned.1.call-done), kind=kOutput, calls=%fused_computation.29 | convolution fusion | flops 805306368 | bytes 8404992 | tf_op jit(solution)/shard_map/dot_general | solution.py:9
  423.9 0.0 copy-start.1
  423.9 1.9 copy-done.1
  425.9 11.6 %fusion.19 = f32[64,256]{1,0:T(8,128)} fusion(f32[64,16384]{1,0:T(8,128)S(1)} %fusion.18, f32[16384,256]{1,0:T(8,128)} %param.5), kind=kOutput, calls=%fused_computation.30 | convolution fusion | flops 3221225472 | bytes 21037056 | tf_op jit(solution)/shard_map/dot_general | solution.py:9
  437.4 0.0 all-reduce.11.cloned.1.call-update
  437.5 2.3 dynamic-slice_multiply_fusion
  439.8 62.8 %all-reduce.11.cloned.1.call-done = f32[64,256]{1,0:T(8,128)} async-done(((f32[64,256]{1,0:T(8,128)}), f32[64,256]{1,0:T(8,128)}) %all-reduce.11.cloned.1.call-update) | async-done | bytes 65552 | tf_op jit(solution)/shard_map/psum | solution.py:27
  502.5 1.1 fusion.20
  503.7 10.3 %psum.55 = f32[64,64]{1,0:T(8,128)S(1)} all-reduce(f32[64,64]{1,0:T(8,128)S(1)} %fusion.20), channel_id=1, replica_groups=mesh['rows'=8,'snaps'=4] {'snaps'}, use_global_device_ids=true, to_apply=%region_8.11 | all-reduce | flops 4096 | bytes 32768 | tf_op jit(solution)/shard_map/psum | solution.py:44
  513.9 0.6 broadcast_multiply_fusion
  514.6 1.5 copy.15
  (4 shorter events, 0.1 us)
Async XLA Ops:
  7.2 0.8 copy-start
  7.2 109.8 %all-reduce.5.cloned.1.call-start = ((), (), s32[]{:S(2)}) async-start(), calls=%async_computation | async-start | bytes 8388608 | tf_op jit(solution)/shard_map/psum | solution.py:39
  28.7 227.1 %all-reduce.7.cloned.1.call-start = ((), (), s32[]{:S(2)}) async-start(), calls=%async_computation.1 | async-start | bytes 131072 | tf_op jit(solution)/shard_map/psum | solution.py:27
  190.6 171.3 %all-reduce.9.cloned.1.call-start = ((), (), s32[]{:S(2)}) async-start(), calls=%async_computation.2 | async-start | bytes 8388608 | tf_op jit(solution)/shard_map/psum | solution.py:39
  276.4 226.2 %all-reduce.11.cloned.1.call-start = ((), (), s32[]{:S(2)}) async-start(), calls=%async_computation.3 | async-start | bytes 131072 | tf_op jit(solution)/shard_map/psum | solution.py:27
  423.9 1.9 copy-start.1
Sparse Core Ops, SparseCore 0:
  28.8 88.1 all-reduce.4
  190.8 64.9 all-reduce.6
  276.5 85.4 all-reduce.8
  437.6 64.9 all-reduce.10
where the time goes:
time: 523 us
  waiting for transfers between devices  301 us (58%)
  matrix products  90.8 us (17%)
  blocking collectives  84.6 us (16%)
  other arithmetic  27.1 us (5%)
  between operations  13.9 us (3%)
    psum x2, waiting for transfers between devices, on_device(): panel = lax.psum(partial_value, 'snaps')  174 us
    psum x2, waiting for transfers between devices, section_whole(): coeffs = lax.psum(product(basis, stress, 1, 0), 'rows')  128 us
    dot_general x9, matrix products, product(): lax.dot_general(left_m, right_m, (((left_dim,), (right_dim,)), ((), ())),...  90.3 us
    psum x2, blocking collectives, section_whole(): factor = inverse_factor(lax.psum(product(panel, panel, 1, 1), 'rows'))  74.3 us
    another operation x6, other arithmetic, inverse_factor(): lower = jnp.linalg.cholesky(gram_total)  13 us
    another operation x4, other arithmetic, inverse_factor(): return lax.linalg.triangular_solve(lower, ident, left_side=True, lower=True)  11.1 us
  transfers between devices with their start and end apart: 4, of which 4 were waited for; matrix products, arithmetic and copies ran while one was open for 0% of the time, Pallas kernels for 0%

commit v1 on v0

--- a/solution.py
+++ b/solution.py
@@ -36,7 +36,10 @@
     basis = None
     for turn in range(2):
         partial_value = product(operand, stress, 1, 1)
-        panel = lax.psum(partial_value, "snaps")
+        peers, panel = (lax.axis_size("snaps"), partial_value)
+        for stride in [1 << k for k in range(peers.bit_length() - 1)]:
+            pairs = [(i, i ^ stride) for i in range(peers)]
+            panel = panel + lax.ppermute(panel, "snaps", pairs)
         basis, operand = section_whole(panel, stress)
     basis = lax.dynamic_slice_in_dim(basis, lax.axis_index("snaps") * share, share, 1)
     scale = math.sqrt(float(rows_dev * lax.axis_size("rows")))

time: 523 us -> 551 us (1.054)
  waiting for transfers between devices: 301 us -> 325 us
  matrix products: 90.8 us -> 78.5 us
  other arithmetic: 27.1 us -> 34.5 us
    ppermute x0 -> x4, waiting for transfers between devices: none -> 196 us  [on_device(): panel = panel + lax.ppermute(panel, 'snaps', pairs)]
    psum x2 -> x0, waiting for transfers between devices: 174 us -> none  [on_device(): panel = lax.psum(partial_value, 'snaps')]
    dot_general x9, matrix products: 90.3 us -> 78 us  [product(): lax.dot_general(left_m, right_m, (((left_dim,), (right_dim,)), ((), ())),...]
    add x0 -> x4, other arithmetic: none -> 7.39 us  [on_device(): panel = panel + lax.ppermute(panel, 'snaps', pairs)]
  transfers between devices with their start and end apart: 4 -> 6, of which waited for: 4 -> 6; matrix products, arithmetic and copies ran while one was open for 0% -> 0% of each run, Pallas kernels for 0% -> 0%
where the time goes in v1:
time: 551 us; the launch traced here: 550 us
  waiting for transfers between devices  325 us (59%)
  blocking collectives  84.1 us (15%)
  matrix products  78.5 us (14%)
  other arithmetic  34.5 us (6%)
  between operations  14.2 us (3%)
  local copies, waits for them, and re-layouts  8.18 us (1%)
    ppermute x4, waiting for transfers between devices, on_device(): panel = panel + lax.ppermute(panel, 'snaps', pairs)  196 us
    psum x2, waiting for transfers between devices, section_whole(): coeffs = lax.psum(product(basis, stress, 1, 0), 'rows')  129 us
    dot_general x9, matrix products, product(): lax.dot_general(left_m, right_m, (((left_dim,), (right_dim,)), ((), ())),...  78 us
    psum x2, blocking collectives, section_whole(): factor = inverse_factor(lax.psum(product(panel, panel, 1, 1), 'rows'))  73.8 us
    another operation x6, other arithmetic, inverse_factor(): lower = jnp.linalg.cholesky(gram_total)  13 us
    another operation x4, other arithmetic, inverse_factor(): return lax.linalg.triangular_solve(lower, ident, left_side=True, lower=True)  11.1 us
  transfers between devices with their start and end apart: 6, of which 6 were waited for; matrix products, arithmetic and copies ran while one was open for 0% of the time, Pallas kernels for 0%

profile of v1, /device:TPU:0, one launch (start us, length us, event | category | flops | bytes accessed | tf_op | source)
XLA Modules:
  0.0 550.2 jit_solution(3900286912524273128)
XLA Ops:
  7.2 0.0 all-reduce.3.cloned.1.call-start
  7.2 0.8 copy-done
  8.0 18.0 %fusion.12 = f32[64,16384]{1,0:T(8,128)S(1)} fusion(f32[64,256]{1,0:T(8,128)S(1)} %copy-done, f32[16384,256]{1,0:T(8,128)} %param.5), kind=kOutput, calls=%fused_computation.23 | convolution fusion | flops 3221225472 | bytes 21037056 | tf_op jit(solution)/shard_map/dot_general | solution.py:9
  26.0 0.5 collective-permute-start
  26.5 6.8 %collective-permute-done = f32[64,16384]{1,0:T(8,128)S(1)} collective-permute-done((f32[64,16384]{1,0:T(8,128)S(1)}, f32[64,16384]{1,0:T(8,128)S(1)}, u32[]{:S(2)}, u32[]{:S(2)}) %collective-permute-start) | collective-permute-done | bytes 4194336 | tf_op jit(solution)/shard_map/ppermute | solution.py:42
  33.3 0.5 add.33
  33.8 2.9 collective-permute-start.1
  36.7 90.9 %collective-permute-done.1 = f32[64,16384]{1,0:T(8,128)S(1)} collective-permute-done((f32[64,16384]{1,0:T(8,128)S(1)}, f32[64,16384]{1,0:T(8,128)S(1)}, u32[]{:S(2)}, u32[]{:S(2)}) %collective-permute-start.1) | collective-permute-done | bytes 4194336 | tf_op jit(solution)/shard_map/ppermute | solution.py:42
  127.6 0.5 add.34
  128.1 1.9 copy-done.2
  130.1 3.4 fusion.13
  133.5 37.7 %psum.35 = f32[64,64]{0,1:T(8,128)S(1)} all-reduce(f32[64,64]{0,1:T(8,128)S(1)} %fusion.13), channel_id=1, replica_groups=mesh['rows'=8,'snaps'=4] {'rows'}, use_global_device_ids=true, to_apply=%region_0.0 | all-reduce | flops 4096 | bytes 32768 | tf_op jit(solution)/shard_map/psum | solution.py:25
  171.2 0.1 copy.6
  171.3 5.8 %cholesky.44 = f32[64,64]{1,0:T(8,128)S(1)} custom-call(f32[64,64]{1,0:T(8,128)S(1)} %fusion.9), custom_call_target="Cholesky" | custom-call | tf_op jit(solution)/shard_map/jit(cholesky)/cholesky | solution.py:19
  177.1 0.6 compare_reduce_fusion.1
  177.8 0.7 fusion.4
  178.5 4.9 custom-call.6
  183.3 0.3 fusion.2
  183.6 5.5 fusion.14
  189.1 11.6 %fusion.15 = f32[64,256]{1,0:T(8,128)} fusion(f32[64,16384]{1,0:T(8,128)S(1)} %fusion.14, f32[16384,256]{1,0:T(8,128)} %param.5), kind=kOutput, calls=%fused_computation.26 | convolution fusion | flops 3221225472 | bytes 21037056 | tf_op jit(solution)/shard_map/dot_general | solution.py:9
  200.7 0.0 all-reduce.3.cloned.1.call-update
  200.7 0.3 all-reduce.5.cloned.1.call-start
  201.0 65.6 %all-reduce.3.cloned.1.call-done = f32[64,256]{1,0:T(8,128)} async-done(((f32[64,256]{1,0:T(8,128)}), f32[64,256]{1,0:T(8,128)}) %all-reduce.3.cloned.1.call-update) | async-done | bytes 65552 | tf_op jit(solution)/shard_map/psum | solution.py:27
  266.5 18.0 %fusion.16 = f32[64,16384]{1,0:T(8,128)S(1)} fusion(f32[64,256]{1,0:T(8,128)} %all-reduce.3.cloned.1.call-done, f32[16384,256]{1,0:T(8,128)} %param.5), kind=kOutput, calls=%fused_computation.27 | convolution fusion | flops 3221225472 | bytes 21037056 | tf_op jit(solution)/shard_map/dot_general | solution.py:9
  284.5 0.1 collective-permute-start.2
  284.6 7.1 %collective-permute-done.2 = f32[64,16384]{1,0:T(8,128)S(1)} collective-permute-done((f32[64,16384]{1,0:T(8,128)S(1)}, f32[64,16384]{1,0:T(8,128)S(1)}, u32[]{:S(2)}, u32[]{:S(2)}) %collective-permute-start.2) | collective-permute-done | bytes 4194336 | tf_op jit(solution)/shard_map/ppermute | solution.py:42
  291.8 2.5 add.35
  294.2 1.5 collective-permute-start.3
  295.7 91.5 %collective-permute-done.3 = f32[64,16384]{1,0:T(8,128)} collective-permute-done((f32[64,16384]{1,0:T(8,128)}, f32[64,16384]{1,0:T(8,128)}, u32[]{:S(2)}, u32[]{:S(2)}) %collective-permute-start.3) | collective-permute-done | bytes 4194336 | tf_op jit(solution)/shard_map/ppermute | solution.py:42
  387.1 3.9 add.36
  391.0 1.9 copy-done.3
  392.9 3.4 fusion.17
  396.4 36.1 %psum.37 = f32[64,64]{0,1:T(8,128)S(1)} all-reduce(f32[64,64]{0,1:T(8,128)S(1)} %fusion.17), channel_id=1, replica_groups=mesh['rows'=8,'snaps'=4] {'rows'}, use_global_device_ids=true, to_apply=%region_4.7 | all-reduce | flops 4096 | bytes 32768 | tf_op jit(solution)/shard_map/psum | solution.py:25
  432.5 0.1 copy.8
  432.6 5.8 %cholesky.55 = f32[64,64]{1,0:T(8,128)S(1)} custom-call(f32[64,64]{1,0:T(8,128)S(1)} %fusion.7), custom_call_target="Cholesky" | custom-call | tf_op jit(solution)/shard_map/jit(cholesky)/cholesky | solution.py:19
  438.5 0.6 compare_reduce_fusion
  439.1 0.7 fusion.5
  439.8 4.9 custom-call.7
  444.7 0.3 fusion
  444.9 5.5 fusion.18
  450.4 1.9 copy-done.4
  452.3 11.6 %fusion.19 = f32[64,256]{1,0:T(8,128)} fusion(f32[64,16384]{1,0:T(8,128)S(1)} %fusion.18, f32[16384,256]{1,0:T(8,128)} %param.5), kind=kOutput, calls=%fused_computation.30 | convolution fusion | flops 3221225472 | bytes 21037056 | tf_op jit(solution)/shard_map/dot_general | solution.py:9
  464.0 2.3 dynamic-slice_multiply_fusion
  466.3 63.6 %all-reduce.5.cloned.1.call-done = f32[64,256]{1,0:T(8,128)} async-done(((f32[64,256]{1,0:T(8,128)}), f32[64,256]{1,0:T(8,128)}) %all-reduce.5.cloned.1.call-update) | async-done | bytes 65552 | tf_op jit(solution)/shard_map/psum | solution.py:27
  529.8 1.1 fusion.20
  530.9 10.3 %psum.39 = f32[64,64]{1,0:T(8,128)S(1)} all-reduce(f32[64,64]{1,0:T(8,128)S(1)} %fusion.20), channel_id=1, replica_groups=mesh['rows'=8,'snaps'=4] {'snaps'}, use_global_device_ids=true, to_apply=%region_6.9 | all-reduce | flops 4096 | bytes 32768 | tf_op jit(solution)/shard_map/psum | solution.py:47
  541.2 0.6 broadcast_multiply_fusion
  541.8 1.5 copy.13
  (11 shorter events, 0.1 us)
Async XLA Ops:
  7.2 0.8 copy-start
  7.2 259.4 %all-reduce.3.cloned.1.call-start = ((), (), s32[]{:S(2)}) async-start(), calls=%async_computation | async-start | bytes 131072 | tf_op jit(solution)/shard_map/psum | solution.py:27
  26.0 7.3 %collective-permute-start = (f32[64,16384]{1,0:T(8,128)S(1)}, f32[64,16384]{1,0:T(8,128)S(1)}, u32[]{:S(2)}, u32[]{:S(2)}) collective-permute-start(f32[64,16384]{1,0:T(8,128)S(1)} %fusion.12), channel_id=1, source_target_pairs={{0,1},{1,0},{2,3},{3,2},{4,5},{5,4},{6,7},{7,6},{8,9},{9,8},{10,11... | collective-permute-start | bytes 12582920 | tf_op jit(solution)/shard_map/ppermute | solution.py:42
  33.8 93.8 %collective-permute-start.1 = (f32[64,16384]{1,0:T(8,128)S(1)}, f32[64,16384]{1,0:T(8,128)S(1)}, u32[]{:S(2)}, u32[]{:S(2)}) collective-permute-start(f32[64,16384]{1,0:T(8,128)S(1)} %add.33), channel_id=1, source_target_pairs={{0,2},{1,3},{2,0},{3,1},{4,6},{5,7},{6,4},{7,5},{8,10},{9,11},{10,... | collective-permute-start | bytes 12582920 | tf_op jit(solution)/shard_map/ppermute | solution.py:42
  128.1 1.9 copy-start.2
  200.7 329.1 %all-reduce.5.cloned.1.call-start = ((), (), s32[]{:S(2)}) async-start(), calls=%async_computation.1 | async-start | bytes 131072 | tf_op jit(solution)/shard_map/psum | solution.py:27
  284.5 7.2 %collective-permute-start.2 = (f32[64,16384]{1,0:T(8,128)S(1)}, f32[64,16384]{1,0:T(8,128)S(1)}, u32[]{:S(2)}, u32[]{:S(2)}) collective-permute-start(f32[64,16384]{1,0:T(8,128)S(1)} %fusion.16), channel_id=1, source_target_pairs={{0,1},{1,0},{2,3},{3,2},{4,5},{5,4},{6,7},{7,6},{8,9},{9,8},{10,11... | collective-permute-start | bytes 12582920 | tf_op jit(solution)/shard_map/ppermute | solution.py:42
  294.2 92.9 %collective-permute-start.3 = (f32[64,16384]{1,0:T(8,128)}, f32[64,16384]{1,0:T(8,128)}, u32[]{:S(2)}, u32[]{:S(2)}) collective-permute-start(f32[64,16384]{1,0:T(8,128)} %add.35), channel_id=1, source_target_pairs={{0,2},{1,3},{2,0},{3,1},{4,6},{5,7},{6,4},{7,5},{8,10},{9,11},{10,... | collective-permute-start | bytes 12582920 | tf_op jit(solution)/shard_map/ppermute | solution.py:42
  391.0 1.9 copy-start.3
  450.4 1.9 copy-start.4
  452.3 91.0 %copy-start.1 = (f32[64,256]{1,0:T(8,128)S(1)}, f32[64,256]{1,0:T(8,128)}, u32[]{:S(2)}) copy-start(f32[64,256]{1,0:T(8,128)} %param.6) | copy-start | bytes 196612
Sparse Core Ops, SparseCore 0:
  200.8 65.6 all-reduce.2
  464.1 65.6 all-reduce.4
